TPU v7x, 32 devices: a whole 2x2x4 slice. The times are simulated.
32 devices in a mesh: parts: 2 (over x), blk: 16 (over z, y, core).
Axes of the slice: x: 2, y: 2, z: 4, core: 2. Of those that a mesh axis runs over, the one named last changes fastest.
Arguments:
- embeddings: bfloat16 [32768, 1024], P(('parts', 'blk')), parts along dimension 0, may hold values from -256 to 256
- owner_ids: int32 [32768, 1], P(('parts', 'blk')), parts along dimension 0, may hold values from 0 to 15, as said below
- local_cluster: int32 [32768], P(('parts', 'blk')), parts along dimension 0, may hold values from 0 to 63
- arrival_rank: int32 [32768], P(('parts', 'blk')), parts along dimension 0, may hold values from 0 to 16383, each once
Outputs:
- scores: float32 [32768], P(('parts', 'blk')), parts along dimension 0
There are 2 independent parts, one for each index of `parts`. A program takes and returns all parts, laid end to end along the dimension named above; each array names one. Nothing has to cross between parts.
Inputs may be any that keep to these rules, and one draw needn't show every extreme that they name: `owner_ids`: in each aligned block of 1024 rows (the rows of one device) no owner is named by more than 128 rows; one owner is named by exactly 128 rows in every block. `arrival_rank`: each of 0 to 16383 appears once.
All inputs are finite; a program needn't handle non-finite values.
Results may differ from a plain program's by a relative error of at most 0.00033.
Values may be sent and summed in bfloat16 or wider, within the bound.
A program may use at most 64 MiB of HBM per device.

v0:
```python
import jax
import jax.numpy as jnp
from jax import lax
from jax.sharding import PartitionSpec as P

CL_DEV = 64


sharpness_divisor = 0.05


def pair_totals(row_units, key_rows_local, col_units, col_keys, all_rows):
    row_groups = key_rows_local // all_rows
    col_groups = col_keys // all_rows
    inner_dot_values = lax.dot_general(
        row_units, col_units, (((1,), (1,)), ((), ())), preferred_element_type=jnp.float32
    )
    pairing_factors = (
        (col_groups[None, :] == row_groups[:, None])
        & (col_keys[None, :] < key_rows_local[:, None])
        & (row_groups[:, None] < CL_DEV)
    )
    return jnp.sum(
        jnp.where(
            pairing_factors,
            jnp.exp(inner_dot_values / sharpness_divisor),
            jnp.zeros_like(inner_dot_values),
        ),
        axis=1,
    )


def per_device(embeddings, owner_ids, local_cluster, arrival_rank):
    row_count, feat_width = embeddings.shape
    peer_count = lax.axis_size("blk")
    capacity = 2 * row_count // peer_count
    slot_total = peer_count * capacity
    all_rows = row_count * peer_count
    wide_rows = embeddings.astype(jnp.float32)
    unit_rows = (
        wide_rows / jnp.sqrt(jnp.sum(wide_rows * wide_rows, axis=1, keepdims=True) + 1e-06)
    ).astype(jnp.bfloat16)
    target = owner_ids[:, 0]
    target_hits = (target[:, None] == jnp.arange(peer_count, dtype=jnp.int32)[None, :]).astype(
        jnp.int32
    )
    earlier = jnp.cumsum(target_hits, axis=0) - target_hits
    position = jnp.sum(earlier * target_hits, axis=1)
    slot_index = target * capacity + position
    sort_key = local_cluster * all_rows + arrival_rank
    vacant_key_slots = CL_DEV * all_rows + jnp.arange(slot_total, dtype=jnp.int32)
    send_units = (
        jnp.zeros((slot_total, feat_width), jnp.bfloat16)
        .at[slot_index]
        .set(unit_rows)
        .reshape(peer_count, capacity, feat_width)
    )
    transmit_key_rows = vacant_key_slots.at[slot_index].set(sort_key).reshape(peer_count, capacity)
    received_entries, got_keys = (
        lax.all_to_all(send_units, "blk", split_axis=0, concat_axis=0, tiled=True),
        lax.all_to_all(transmit_key_rows, "blk", split_axis=0, concat_axis=0, tiled=True),
    )
    flat_units = received_entries.reshape(slot_total, feat_width)
    flat_keys = got_keys.reshape(slot_total)
    block_rows = min(512, slot_total)
    fragment_list = []
    for offset in range(0, slot_total, block_rows):
        fragment_list.append(
            pair_totals(
                flat_units[offset : offset + block_rows],
                flat_keys[offset : offset + block_rows],
                flat_units,
                flat_keys,
                all_rows,
            )
        )
    totals = jnp.concatenate(fragment_list, axis=0)
    slot_scores = jnp.log1p(totals).reshape(peer_count, capacity)
    returned = lax.all_to_all(slot_scores, "blk", split_axis=0, concat_axis=0, tiled=True)
    return returned.reshape(slot_total)[slot_index]


def solution(mesh):
    return jax.shard_map(
        per_device,
        mesh=mesh,
        in_specs=(
            P(("parts", "blk"), None),
            P(("parts", "blk"), None),
            P(("parts", "blk")),
            P(("parts", "blk")),
        ),
        out_specs=P(("parts", "blk")),
        check_vma=False,
    )
```

profile of v0, /device:TPU:0, one launch (start us, length us, event | category | flops | bytes accessed | tf_op | source)
XLA Modules:
  0.0 177.4 jit_solution(15196833902464177144)
XLA Ops:
  0.0 0.6 iota_add_fusion
  0.6 0.7 fusion.9
  1.3 4.5 %reduce-window.6 = s32[16,8,128]{2,1,0:T(8,128)S(1)} reduce-window(s32[16,8,128]{2,1,0:T(8,128)S(1)} %fusion.9, s32[]{:T(128)} %constant.69.clone.1), window={size=1x1x128 pad=0_0x0_0x127_0}, to_apply=%region_0.0 | reduce-window | flops 2080768 | bytes 131076 | tf_op jit(solution)/shard_map/reduce-window
  5.8 0.1 slice.78
  5.9 0.1 copy.7
  6.1 0.1 broadcast_add_fusion
  6.2 0.7 fusion.8
  6.9 0.7 compare_select_fusion
  7.6 0.7 multiply_add_fusion
  8.3 5.7 %scatter_fusion = s32[2048]{0:T(1024)} fusion(s32[2048]{0:T(1024)} %iota_add_fusion, s32[1024]{0:T(1024)S(1)} %bitcast.59, s32[1024]{0:T(1024)S(1)} %multiply_add_fusion), kind=kCustom, calls=%fused_computation.1 | custom fusion | bytes 16384 | tf_op jit(solution)/shard_map/scatter | solution.py:58
  14.1 7.4 %all-to-all-start = ((s32[16,1,128]{2,1,0:T(1,128)}), s32[16,1,128]{2,1,0:T(1,128)S(1)}, u32[]{:S(2)}, u32[]{:S(2)}) async-start(s32[16,1,128]{2,1,0:T(1,128)} %bitcast.6), calls=%async_computation | async-start | bytes 16384 | tf_op jit(solution)/shard_map/all_to_all | solution.py:61
  21.5 0.5 fusion
  22.0 8.3 %scatter_custom_fusion.1 = bf16[2048,1024]{1,0:T(8,128)(2,1)} fusion(s32[1024]{0:T(1024)S(1)} %bitcast.60, bf16[1024,1024]{1,0:T(8,128)(2,1)S(1)} %copy-done, f32[1024]{0:T(1024)S(1)} %add_sqrt_fusion, bf16[]{:T(256)} %constant.77.clone.1), kind=kCustom, calls=%fused_computation.11 | custom fusion | flops 3145728 | bytes 6295554 | tf_op jit(solution)/shard_map/scatter | solution.py:55
  30.3 6.1 %all-to-all-start.1 = ((bf16[16,128,1024]{2,1,0:T(8,128)(2,1)}), bf16[16,128,1024]{2,1,0:T(8,128)(2,1)}, u32[]{:S(2)}, u32[]{:S(2)}) async-start(bf16[16,128,1024]{2,1,0:T(8,128)(2,1)} %bitcast.48), calls=%async_computation.1 | async-start | bytes 8388608 | tf_op jit(solution)/shard_map/all_to_all | solution.py:60
  36.4 77.6 %all-to-all-done.1 = bf16[16,128,1024]{2,1,0:T(8,128)(2,1)} async-done(((bf16[16,128,1024]{2,1,0:T(8,128)(2,1)}), bf16[16,128,1024]{2,1,0:T(8,128)(2,1)}, u32[]{:S(2)}, u32[]{:S(2)}) %all-to-all-start.1) | async-done | bytes 4194336 | tf_op jit(solution)/shard_map/all_to_all | solution.py:60
  114.0 2.7 %fusion.20 = (bf16[4,128,1024]{2,1,0:T(8,128)(2,1)S(1)}, bf16[4,128,1024]{2,1,0:T(8,128)(2,1)S(1)}, bf16[4,128,1024]{2,1,0:T(8,128)(2,1)S(1)}, bf16[4,128,1024]{2,1,0:T(8,128)(2,1)S(1)}) fusion(bf16[16,128,1024]{2,1,0:T(8,128)(2,1)} %all-to-all-done.1), kind=kLoop, calls=%fused_computation.67 | loop fusion | bytes 8388608 | tf_op jit(solution)/shard_map/slice | solution.py:70
  116.7 5.9 %select_reduce_fusion = f32[512]{0:T(512)S(1)} fusion(bf16[512,1024]{1,0:T(8,128)(2,1)S(1)} %bitcast.52, bf16[2048,1024]{1,0:T(8,128)(2,1)} %bitcast.11, s32[2048]{0:T(1024)S(1)} %bitcast.55, s32[2048]{0:T(1024)S(1)} %add_select_fusion, s32[512]{0:T(512)S(1)} %bitcast.73, s32[512]{0:T(512)S(1)} %get-tuple-element.12, pred[512]{0:T(512)(128)(4,1)S(1)} %get-tuple-element.11), kind=kOutput, calls=%fused_computation.7 | convolution fusion | flops 2154823168 | bytes 5265920 | tf_op jit(solution)/shard_map/dot_general | solution.py:15
  122.5 5.9 %select_reduce_fusion.1 = f32[512]{0:T(512)S(1)} fusion(bf16[512,1024]{1,0:T(8,128)(2,1)S(1)} %bitcast.51, bf16[2048,1024]{1,0:T(8,128)(2,1)} %bitcast.11, s32[2048]{0:T(1024)S(1)} %bitcast.56, s32[2048]{0:T(1024)S(1)} %add_select_fusion, s32[512]{0:T(512)S(1)} %bitcast.71, s32[512]{0:T(512)S(1)} %get-tuple-element.10, pred[512]{0:T(512)(128)(4,1)S(1)} %get-tuple-element.9), kind=kOutput, calls=%fused_computation.8 | convolution fusion | flops 2154823168 | bytes 5265920 | tf_op jit(solution)/shard_map/dot_general | solution.py:15
  128.4 5.9 %select_reduce_fusion.2 = f32[512]{0:T(512)S(1)} fusion(bf16[512,1024]{1,0:T(8,128)(2,1)S(1)} %bitcast.50, bf16[2048,1024]{1,0:T(8,128)(2,1)} %bitcast.11, s32[2048]{0:T(1024)S(1)} %bitcast.57, s32[2048]{0:T(1024)S(1)} %add_select_fusion, s32[512]{0:T(512)S(1)} %bitcast.69, s32[512]{0:T(512)S(1)} %get-tuple-element.8, pred[512]{0:T(512)(128)(4,1)S(1)} %get-tuple-element.7), kind=kOutput, calls=%fused_computation.9 | convolution fusion | flops 2154823168 | bytes 5265920 | tf_op jit(solution)/shard_map/dot_general | solution.py:15
  134.3 5.9 %select_reduce_fusion.3 = f32[512]{0:T(512)S(1)} fusion(bf16[512,1024]{1,0:T(8,128)(2,1)S(1)} %bitcast.49, bf16[2048,1024]{1,0:T(8,128)(2,1)} %bitcast.11, s32[2048]{0:T(1024)S(1)} %bitcast.58, s32[2048]{0:T(1024)S(1)} %add_select_fusion, s32[512]{0:T(512)S(1)} %bitcast.67, s32[512]{0:T(512)S(1)} %get-tuple-element.6, pred[512]{0:T(512)(128)(4,1)S(1)} %get-tuple-element.5), kind=kOutput, calls=%fused_computation.10 | convolution fusion | flops 2154823168 | bytes 5265920 | tf_op jit(solution)/shard_map/dot_general | solution.py:15
  140.1 0.6 maximum_log-plus-one_fusion
  140.8 19.6 %all-to-all-start.2 = ((f32[16,1,128]{2,1,0:T(1,128)}), f32[16,1,128]{2,1,0:T(1,128)S(1)}, u32[]{:S(2)}, u32[]{:S(2)}) async-start(f32[16,1,128]{2,1,0:T(1,128)} %maximum_log-plus-one_fusion), calls=%async_computation.2 | async-start | bytes 16384 | tf_op jit(solution)/shard_map/all_to_all | solution.py:79
  160.4 6.4 %all-to-all-done.2 = f32[16,1,128]{2,1,0:T(1,128)S(1)} async-done(((f32[16,1,128]{2,1,0:T(1,128)}), f32[16,1,128]{2,1,0:T(1,128)S(1)}, u32[]{:S(2)}, u32[]{:S(2)}) %all-to-all-start.2) | async-done | bytes 8224 | tf_op jit(solution)/shard_map/all_to_all | solution.py:79
  166.8 10.5 %gather_fusion = f32[1024]{0:T(1024)} fusion(f32[2048]{0:T(1024)S(1)} %bitcast.47, s32[1024]{0:T(1024)S(1)} %broadcast_clamp_fusion), kind=kCustom, calls=%fused_computation | custom fusion | bytes 12288 | tf_op jit(solution)/shard_map/gather | solution.py:80
  (14 shorter events, 0.2 us)
Async XLA Ops:
  8.3 13.1 %copy-start = (bf16[1024,1024]{1,0:T(8,128)(2,1)S(1)}, bf16[1024,1024]{1,0:T(8,128)(2,1)}, u32[]{:S(2)}) copy-start(bf16[1024,1024]{1,0:T(8,128)(2,1)} %param.4) | copy-start | bytes 6291460
  14.1 16.2 %all-to-all-start = ((s32[16,1,128]{2,1,0:T(1,128)}), s32[16,1,128]{2,1,0:T(1,128)S(1)}, u32[]{:S(2)}, u32[]{:S(2)}) async-start(s32[16,1,128]{2,1,0:T(1,128)} %bitcast.6), calls=%async_computation | async-start | bytes 16384 | tf_op jit(solution)/shard_map/all_to_all | solution.py:61
  30.3 83.7 %all-to-all-start.1 = ((bf16[16,128,1024]{2,1,0:T(8,128)(2,1)}), bf16[16,128,1024]{2,1,0:T(8,128)(2,1)}, u32[]{:S(2)}, u32[]{:S(2)}) async-start(bf16[16,128,1024]{2,1,0:T(8,128)(2,1)} %bitcast.48), calls=%async_computation.1 | async-start | bytes 8388608 | tf_op jit(solution)/shard_map/all_to_all | solution.py:60
  140.8 26.1 %all-to-all-start.2 = ((f32[16,1,128]{2,1,0:T(1,128)}), f32[16,1,128]{2,1,0:T(1,128)S(1)}, u32[]{:S(2)}, u32[]{:S(2)}) async-start(f32[16,1,128]{2,1,0:T(1,128)} %maximum_log-plus-one_fusion), calls=%async_computation.2 | async-start | bytes 16384 | tf_op jit(solution)/shard_map/all_to_all | solution.py:79
where the time goes:
time: 178 us; the launch traced here: 177 us
  waiting for transfers between devices  84 us (47%)
  starting transfers between devices  33.1 us (19%)
  matrix products  23.5 us (13%)
  local copies, waits for them, and re-layouts  19.2 us (11%)
  other arithmetic  17.5 us (10%)
    all_to_all x1, waiting for transfers between devices, per_device(): lax.all_to_all(send_units, 'blk', split_axis=0, concat_axis=0, tiled=True)  77.6 us
    dot_general x4, matrix products, pair_totals(): lax.dot_general(row_units, col_units, (((1,), (1,)), ((), ())), preferred...  23.5 us
    all_to_all x1, starting transfers between devices, per_device(): lax.all_to_all(slot_scores, 'blk', split_axis=0, concat_axis=0, tiled=True)  19.6 us
    gather x1, local copies, waits for them, and re-layouts, per_device(): return returned.reshape(slot_total)[slot_index]  10.5 us
    scatter x1, other arithmetic, per_device(): send_units = jnp.zeros((slot_total, feat_width), jnp.bfloat16).at[slot_in...  8.3 us
    all_to_all x1, starting transfers between devices, per_device(): lax.all_to_all(transmit_key_rows, 'blk', split_axis=0, concat_axis=0, til...  7.39 us
    all_to_all x1, waiting for transfers between devices, per_device(): lax.all_to_all(slot_scores, 'blk', split_axis=0, concat_axis=0, tiled=True)  6.39 us
    all_to_all x1, starting transfers between devices, per_device(): lax.all_to_all(send_units, 'blk', split_axis=0, concat_axis=0, tiled=True)  6.07 us
  transfers between devices with their start and end apart: 3, of which 2 were waited for; matrix products, arithmetic and copies ran while one was open for 5% of the time, Pallas kernels for 0%

commit v1 on v0

v1 whole, which is shorter than its diff:
```python
import functools

import jax
import jax.numpy as jnp
from jax import lax
from jax.experimental import pallas as pl
from jax.experimental.pallas import tpu as pltpu
from jax.sharding import PartitionSpec as P

CL_DEV = 64
SLOTS = 128
PAIR = 2 * SLOTS
SHARPNESS = 20.0 * 1.4426950408889634


def dot_nt(a, b):
    return lax.dot_general(a, b, (((1,), (1,)), ((), ())), preferred_element_type=jnp.float32)


def kernel(
    n, emb, tgt, lc, rank, out,
    unit, send, recv, ksend, krecv, rowacc, ssend, ret,
    us, ur, ks, kr, rs, rr,
):
    rows = emb.shape[0]
    all_rows = rows * n
    nc = n // 2
    me = lax.axis_index("blk")
    mine = me // 2
    mate = me + 1 - 2 * (me % 2)

    barrier = pltpu.get_barrier_semaphore()

    def greet(k, _):
        pl.semaphore_signal(
            barrier, inc=1, device_id={"blk": (me + k) % n}, device_id_type=pl.DeviceIdType.MESH
        )
        return 0

    lax.fori_loop(1, n, greet, 0)

    def normalise(i, _):
        span = pl.ds(pl.multiple_of(i * 128, 128), 128)
        wide = emb[span, :].astype(jnp.float32)
        inv = 1.0 / jnp.sqrt(jnp.sum(wide * wide, axis=1, keepdims=True) + 1e-06)
        unit[span, :] = (wide * inv).astype(jnp.bfloat16)
        return 0

    lax.fori_loop(0, rows // 128, normalise, 0)

    target = tgt[...]
    hits = target == lax.broadcasted_iota(jnp.int32, (n, rows), 0)
    before = (
        lax.broadcasted_iota(jnp.int32, (rows, rows), 0)
        < lax.broadcasted_iota(jnp.int32, (rows, rows), 1)
    )
    hits_f = hits.astype(jnp.float32)
    earlier = jnp.dot(
        hits_f.astype(jnp.bfloat16),
        before.astype(jnp.float32).astype(jnp.bfloat16),
        preferred_element_type=jnp.float32,
    )
    pos = jnp.sum(hits_f * earlier, axis=0, keepdims=True).astype(jnp.int32)
    slot = target * SLOTS + pos
    at_slot = pos == lax.broadcasted_iota(jnp.int32, (SLOTS, rows), 0)
    at_slot_b = at_slot.astype(jnp.float32).astype(jnp.bfloat16)

    rank_v = rank[...]
    rank_hi = rank_v // 256
    rank_lo = rank_v - rank_hi * 256
    parts = [
        hits_f,
        hits_f * lc[...].astype(jnp.float32),
        hits_f * rank_hi.astype(jnp.float32),
        hits_f * rank_lo.astype(jnp.float32),
    ]
    table = [dot_nt(p.astype(jnp.bfloat16), at_slot_b) for p in parts]
    base = (table[1] + (1.0 - table[0]) * float(CL_DEV)) * float(all_rows)
    key = base + table[2] * 256.0 + table[3]
    top = lax.broadcasted_iota(jnp.int32, (n, 8, SLOTS), 1) < 4
    ksend[...] = jnp.where(top, key[:, None, :], base[:, None, :])

    def key_copy(src, dst, send_at, recv_at, dev):
        return pltpu.make_async_remote_copy(
            src_ref=ksend.at[src], dst_ref=krecv.at[dst],
            send_sem=ks.at[send_at], recv_sem=kr.at[recv_at],
            device_id={"blk": dev}, device_id_type=pl.DeviceIdType.MESH,
        )

    def unit_copy(src, dst, send_at, recv_at, dev):
        return pltpu.make_async_remote_copy(
            src_ref=send.at[src], dst_ref=recv.at[dst],
            send_sem=us.at[send_at], recv_sem=ur.at[recv_at],
            device_id={"blk": dev}, device_id_type=pl.DeviceIdType.MESH,
        )

    def score_copy(src, dst, send_at, recv_at, dev):
        return pltpu.make_async_remote_copy(
            src_ref=ssend.at[src], dst_ref=ret.at[dst],
            send_sem=rs.at[send_at], recv_sem=rr.at[recv_at],
            device_id={"blk": dev}, device_id_type=pl.DeviceIdType.MESH,
        )

    pl.semaphore_wait(barrier, n - 1)

    def packed(chip):
        want = chip * PAIR + lax.broadcasted_iota(jnp.int32, (PAIR, rows), 0)
        pick = (slot == want).astype(jnp.float32).astype(jnp.bfloat16)
        moved = jnp.dot(pick, unit[...], preferred_element_type=jnp.float32)
        return moved.astype(jnp.bfloat16).reshape(2, SLOTS, emb.shape[1])

    def dispatch(j, _):
        off = nc // 2 + ((j + 1) // 2) * (1 - 2 * (j % 2))
        chip = (mine + off + nc) % nc
        send[pl.ds(2 * chip, 2)] = packed(chip)
        for h in range(2):
            d = 2 * chip + h
            unit_copy(d, me, d, me, d).start()
            key_copy(d, me, d, me, d).start()
        return 0

    lax.fori_loop(0, nc - 1, dispatch, 0)
    send[pl.ds(2 * mine, 2)] = packed(mine)
    unit_copy(mate, me, mate, me, mate).start()
    key_copy(mate, me, mate, me, mate).start()
    recv[me] = send[me]
    krecv[me] = ksend[me]

    def group_at(t):
        off = ((t + 1) // 2) * (2 * (t % 2) - 1)
        return (mine + off + nc) % nc

    def block(t_units, g):
        return jnp.exp2(
            dot_nt(t_units, recv[pl.ds(2 * g, 2)].reshape(PAIR, emb.shape[1])) * SHARPNESS
        )

    def key_rows(g):
        first, second = krecv[2 * g], krecv[2 * g + 1]
        both = jnp.concatenate([first, second], axis=1)
        return both[0:1], both[4:5]

    def fold(x):
        return x[:, :SLOTS] + x[:, SLOTS:]

    def step(t, _):
        g = group_at(t)
        for h in range(2):
            s = 2 * g + h

            @pl.when(s != me)
            def _():
                key_copy(s, s, s, s, s).wait_recv()
                unit_copy(s, s, s, s, s).wait_recv()

        krow, brow = key_rows(g)
        kc = jnp.transpose(jnp.broadcast_to(krow, (SLOTS, PAIR)))
        bc = jnp.transpose(jnp.broadcast_to(brow, (SLOTS, PAIR)))
        kc = jnp.concatenate([kc, kc], axis=1)
        bc = jnp.concatenate([bc, bc], axis=1)
        mine_units = recv[pl.ds(2 * g, 2)].reshape(PAIR, emb.shape[1])
        e = block(mine_units, g)
        acc = fold(jnp.where((bc == brow) & (krow < kc), e, 0.0))

        def against(u, acc):
            gu = group_at(u)
            kru, bru = key_rows(gu)
            e = jnp.where(bc == bru, block(mine_units, gu), 0.0)
            lower = jnp.where(kru < kc, e, 0.0)
            upper = (e - lower).reshape(PAIR // 8, 8, PAIR).sum(axis=0)
            rowacc[u] = rowacc[u] + upper
            return acc + fold(lower)

        acc = lax.fori_loop(0, t, against, acc)
        total = jnp.broadcast_to(jnp.sum(acc, axis=1, keepdims=True), (PAIR, SLOTS))
        as_row = jnp.transpose(total)[0:8, :]
        first = lax.broadcasted_iota(jnp.int32, (8, PAIR), 0) == 0
        rowacc[t] = jnp.where(first, as_row, 0.0)
        return 0

    lax.fori_loop(0, nc, step, 0)

    def give_back(t, _):
        g = group_at(t)
        scores = jnp.log1p(jnp.sum(rowacc[t], axis=0, keepdims=True))
        for h in range(2):
            s = 2 * g + h
            ssend[s] = jnp.broadcast_to(scores[:, h * SLOTS : (h + 1) * SLOTS], (8, SLOTS))

            @pl.when(s != me)
            def _():
                score_copy(s, me, s, me, s).start()

        return 0

    lax.fori_loop(0, nc, give_back, 0)
    ret[me] = ssend[me]

    def collect(k, _):
        s = (me + k) % n
        score_copy(s, s, s, s, s).wait_recv()
        return 0

    lax.fori_loop(1, n, collect, 0)

    back = ret[...][:, 0, :]
    hits_b = hits_f.astype(jnp.bfloat16)
    hi = back.astype(jnp.bfloat16)
    rest = back - hi.astype(jnp.float32)
    mid = rest.astype(jnp.bfloat16)
    low = (rest - mid.astype(jnp.float32)).astype(jnp.bfloat16)
    spread = sum(
        lax.dot_general(p, hits_b, (((0,), (0,)), ((), ())), preferred_element_type=jnp.float32)
        for p in (hi, mid, low)
    )
    out[...] = jnp.sum(jnp.where(at_slot, spread, 0.0), axis=0, keepdims=True)

    def drain(k, _):
        s = (me + k) % n
        unit_copy(s, s, s, s, s).wait_send()
        key_copy(s, s, s, s, s).wait_send()
        score_copy(s, s, s, s, s).wait_send()
        return 0

    lax.fori_loop(1, n, drain, 0)


def per_device(embeddings, owner_ids, local_cluster, arrival_rank):
    rows, width = embeddings.shape
    n = lax.axis_size("blk")
    nc = n // 2
    vmem = pl.BlockSpec(memory_space=pltpu.VMEM)
    dma = pltpu.SemaphoreType.DMA((n,))
    scores = pl.pallas_call(
        functools.partial(kernel, n),
        out_shape=jax.ShapeDtypeStruct((1, rows), jnp.float32),
        in_specs=[vmem] * 4,
        out_specs=vmem,
        scratch_shapes=[
            pltpu.VMEM((rows, width), jnp.bfloat16),
            pltpu.VMEM((n, SLOTS, width), jnp.bfloat16),
            pltpu.VMEM((n, SLOTS, width), jnp.bfloat16),
            pltpu.VMEM((n, 8, SLOTS), jnp.float32),
            pltpu.VMEM((n, 8, SLOTS), jnp.float32),
            pltpu.VMEM((nc, 8, PAIR), jnp.float32),
            pltpu.VMEM((n, 8, SLOTS), jnp.float32),
            pltpu.VMEM((n, 8, SLOTS), jnp.float32),
            dma, dma, dma, dma, dma, dma,
        ],
        compiler_params=pltpu.CompilerParams(
            collective_id=0, has_side_effects=True, vmem_limit_bytes=56 * 1024 * 1024
        ),
    )(
        embeddings,
        owner_ids.reshape(1, rows),
        local_cluster.reshape(1, rows),
        arrival_rank.reshape(1, rows),
    )
    return scores.reshape(rows)


def solution(mesh):
    return jax.shard_map(
        per_device,
        mesh=mesh,
        in_specs=(
            P(("parts", "blk"), None),
            P(("parts", "blk"), None),
            P(("parts", "blk")),
            P(("parts", "blk")),
        ),
        out_specs=P(("parts", "blk")),
        check_vma=False,
    )
```

time: 178 us -> 122 us (0.69)
  Pallas kernels: 0 us -> 121 us
  waiting for transfers between devices: 84 us -> 0 us
  starting transfers between devices: 33.1 us -> 0 us
  matrix products: 23.5 us -> 0 us
  local copies, waits for them, and re-layouts: 19.2 us -> 1.28 us
  other arithmetic: 17.5 us -> 0 us
    pallas_call x0 -> x1, Pallas kernels: none -> 121 us  [per_device(): pl.pallas_call(functools.partial(kernel, n), out_shape=jax.ShapeDtypeStru...]
    all_to_all x3 -> x0, waiting for transfers between devices: 84 us -> none  [the longest x1 77.6 us: per_device(): lax.all_to_all(send_units, 'blk', split_axis=0, concat_axis=0, tiled=True)]
    all_to_all x3 -> x0, starting transfers between devices: 33.1 us -> none  [the longest x1 19.6 us: per_device(): lax.all_to_all(slot_scores, 'blk', split_axis=0, concat_axis=0, tiled=True)]
    dot_general x4 -> x0, matrix products: 23.5 us -> none  [pair_totals(): lax.dot_general(row_units, col_units, (((1,), (1,)), ((), ())), preferred...]
    gather x1 -> x0, local copies, waits for them, and re-layouts: 10.5 us -> none  [per_device(): return returned.reshape(slot_total)[slot_index]]
    scatter x1 -> x0, other arithmetic: 8.3 us -> none  [per_device(): send_units = jnp.zeros((slot_total, feat_width), jnp.bfloat16).at[slot_in...]
    scatter x1 -> x0, local copies, waits for them, and re-layouts: 5.72 us -> none  [per_device(): vacant_key_slots.at[slot_index].set(sort_key).reshape(peer_count, capacity)]
    another operation x3 -> x0, other arithmetic: 4.61 us -> none
  transfers between devices with their start and end apart: 3 -> 0, of which waited for: 2 -> 0; matrix products, arithmetic and copies ran while one was open for 5% -> 0% of each run, Pallas kernels for 0% -> 0%
where the time goes in v1:
time: 122 us
  Pallas kernels  121 us (99%)
  local copies, waits for them, and re-layouts  1.28 us (1%)
    pallas_call x1, Pallas kernels, per_device(): pl.pallas_call(functools.partial(kernel, n), out_shape=jax.ShapeDtypeStru...  121 us

profile of v1, /device:TPU:0, one launch (start us, length us, event | category | flops | bytes accessed | tf_op | source)
XLA Modules:
  0.0 122.2 jit_solution(7889543391076330204)
XLA Ops:
  0.0 120.9 %shard_map.46 = f32[1,1024]{1,0:T(1,128)} custom-call(bf16[1024,1024]{1,0:T(8,128)(2,1)} %emb.1, s32[1,1024]{1,0:T(1,128)} %bitcast.5, s32[1,1024]{1,0:T(1,128)} %bitcast.6, s32[1,1024]{1,0:T(1,128)} %bitcast.7), custom_call_target="tpu_custom_call" | custom-call | tf_op jit(solution)/shard_map/pallas_call | solution.py:234
  120.9 1.3 %copy.6 = f32[1024]{0:T(1024)} copy(f32[1024]{0:T(1024)} %bitcast.4) | data formatting | bytes 8192

commit v2 on v1

v2 whole, which is shorter than its diff:
```python
import functools

import jax
import jax.numpy as jnp
from jax import lax
from jax.experimental import pallas as pl
from jax.experimental.pallas import tpu as pltpu
from jax.sharding import PartitionSpec as P

CL_DEV = 64
LANES = 128
MESH = pl.DeviceIdType.MESH
SHARPNESS = 20.0 * 1.4426950408889634


def dot_nt(a, b):
    return lax.dot_general(a, b, (((1,), (1,)), ((), ())), preferred_element_type=jnp.float32)


def one_hot(ids, count):
    hits = ids == lax.broadcasted_iota(jnp.int32, (count, ids.shape[1]), 0)
    return hits, hits.astype(jnp.float32)


def narrow(x):
    return x.astype(jnp.bfloat16)


def below(count):
    first = lax.broadcasted_iota(jnp.int32, (count, count), 0)
    return first < lax.broadcasted_iota(jnp.int32, (count, count), 1)


def exact_dot(a, b):
    total = 0.0
    for _ in range(3):
        total = total + jnp.dot(narrow(a), b, preferred_element_type=jnp.float32)
        a = a - narrow(a).astype(jnp.float32)
    return total


def plan(n, groups, emb, own, lc, unit, tgt, most, cnt, tops, cs, cr, ts, tr):
    rows = emb.shape[0]
    me = lax.axis_index("blk")
    part = lax.axis_index("parts")

    barrier = pltpu.get_barrier_semaphore()

    def greet(k, _):
        pl.semaphore_signal(
            barrier, inc=1, device_id={"blk": (me + k) % n}, device_id_type=MESH
        )
        return 0

    lax.fori_loop(1, n, greet, 0)
    for k in range(1, groups):
        pl.semaphore_signal(
            barrier, inc=1, device_id={"parts": (part + k) % groups}, device_id_type=MESH
        )

    _, owner_f = one_hot(own[...], n)
    local, local_f = one_hot(lc[...], LANES)
    cnt[me] = dot_nt(narrow(owner_f), narrow(local_f))
    pl.semaphore_wait(barrier, n - 1 + groups - 1)

    def count_copy(src, dst, at, dev):
        return pltpu.make_async_remote_copy(
            src_ref=cnt.at[src], dst_ref=cnt.at[dst], send_sem=cs.at[at], recv_sem=cr.at[dst],
            device_id={"blk": dev}, device_id_type=MESH,
        )

    def send_counts(k, _):
        d = (me + k) % n
        count_copy(me, me, d, d).start()
        return 0

    lax.fori_loop(1, n, send_counts, 0)

    def normalise(i, _):
        span = pl.ds(pl.multiple_of(i * 128, 128), 128)
        wide = emb[span, :].astype(jnp.float32)
        inv = 1.0 / jnp.sqrt(jnp.sum(wide * wide, axis=1, keepdims=True) + 1e-06)
        unit[span, :] = narrow(wide * inv)
        return 0

    lax.fori_loop(0, rows // 128, normalise, 0)

    def take_counts(k, _):
        s = (me + k) % n
        count_copy(s, s, s, s).wait_recv()
        return 0

    lax.fori_loop(1, n, take_counts, 0)

    total = jnp.sum(cnt[...], axis=0)
    inside = exact_dot(total, narrow(below(LANES).astype(jnp.float32)))
    sums = jnp.broadcast_to(jnp.sum(total, axis=1, keepdims=True), (n, LANES))
    ahead = jnp.zeros((n, LANES), jnp.float32)
    line = lax.broadcasted_iota(jnp.int32, (n, LANES), 0)
    for o in range(n - 1):
        ahead = ahead + jnp.where(line > o, sums[o : o + 1], 0.0)
    middle = inside + ahead + 0.5 * total
    dest = jnp.minimum(jnp.floor(middle * (1.0 / rows)), float(n - 1))

    def widest(d, top):
        mask = (dest == d.astype(jnp.float32)).astype(jnp.float32)
        per_src = jnp.sum(cnt[...] * mask[None], axis=1)
        return jnp.maximum(top, jnp.sum(per_src, axis=1, keepdims=True))

    top = lax.fori_loop(0, n, widest, jnp.zeros((n, 1), jnp.float32))
    top = jnp.broadcast_to(jnp.max(top, axis=0, keepdims=True), (8, LANES))

    tops[part] = top

    def top_copy(src, dst, at, dev):
        return pltpu.make_async_remote_copy(
            src_ref=tops.at[src], dst_ref=tops.at[dst], send_sem=ts.at[at], recv_sem=tr.at[dst],
            device_id={"parts": dev}, device_id_type=MESH,
        )

    others = [(part + k) % groups for k in range(1, groups)]
    for d in others:
        top_copy(part, part, d, d).start()

    spread = lax.dot_general(
        narrow(dest), narrow(owner_f), (((0,), (0,)), ((), ())), preferred_element_type=jnp.float32
    )
    tgt[...] = jnp.sum(jnp.where(local, spread, 0.0), axis=0, keepdims=True).astype(jnp.int32)

    for d in others:
        top_copy(d, d, d, d).wait_recv()
    most[...] = jnp.max(tops[...], axis=0)
    for d in others:
        top_copy(d, d, d, d).wait_send()

    def drain(k, _):
        d = (me + k) % n
        count_copy(d, d, d, d).wait_send()
        return 0

    lax.fori_loop(1, n, drain, 0)


def kernel(
    n, SLOTS, q, unit, tgt, own, lc, rank, out,
    send, recv, ksend, krecv, krow, brow, rowacc, ssend, ret,
    us, ur, ks, kr, rs, rr,
):
    rows, width = unit.shape
    nc = n // 2
    ng = n // q
    PAIR = 2 * SLOTS
    span = q * SLOTS
    me = lax.axis_index("blk")
    mine = me // 2
    home = me // q
    mate = me + 1 - 2 * (me % 2)

    barrier = pltpu.get_barrier_semaphore()

    def greet(k, _):
        pl.semaphore_signal(
            barrier, inc=1, device_id={"blk": (me + k) % n}, device_id_type=MESH
        )
        return 0

    lax.fori_loop(1, n, greet, 0)

    target = tgt[...]
    _, hits_f = one_hot(target, n)
    earlier = jnp.dot(
        narrow(hits_f), narrow(below(rows).astype(jnp.float32)), preferred_element_type=jnp.float32
    )
    pos = jnp.sum(hits_f * earlier, axis=0, keepdims=True).astype(jnp.int32)
    slot = target * SLOTS + pos
    at_slot, at_slot_f = one_hot(pos, LANES)

    rank_v = rank[...]
    rank_hi = rank_v // 256
    rank_lo = rank_v - rank_hi * 256
    parts = [hits_f] + [
        hits_f * v.astype(jnp.float32) for v in (own[...], lc[...], rank_hi, rank_lo)
    ]
    table = [dot_nt(narrow(p), narrow(at_slot_f)) for p in parts]
    cluster = table[1] * float(CL_DEV) + table[2] + table[0] - 1.0
    order = table[3] * 256.0 + table[4]
    top = lax.broadcasted_iota(jnp.int32, (n, 8, LANES), 1) < 4
    ksend[...] = jnp.where(top, order[:, None, :], cluster[:, None, :])

    def key_copy(src, dst, send_at, recv_at, dev):
        return pltpu.make_async_remote_copy(
            src_ref=ksend.at[src], dst_ref=krecv.at[dst],
            send_sem=ks.at[send_at], recv_sem=kr.at[recv_at],
            device_id={"blk": dev}, device_id_type=MESH,
        )

    def unit_copy(src, dst, send_at, recv_at, dev):
        return pltpu.make_async_remote_copy(
            src_ref=send.at[src], dst_ref=recv.at[dst],
            send_sem=us.at[send_at], recv_sem=ur.at[recv_at],
            device_id={"blk": dev}, device_id_type=MESH,
        )

    def score_copy(src, dst, send_at, recv_at, dev):
        return pltpu.make_async_remote_copy(
            src_ref=ssend.at[src], dst_ref=ret.at[dst],
            send_sem=rs.at[send_at], recv_sem=rr.at[recv_at],
            device_id={"blk": dev}, device_id_type=MESH,
        )

    pl.semaphore_wait(barrier, n - 1)

    def packed(chip):
        want = chip * PAIR + lax.broadcasted_iota(jnp.int32, (PAIR, rows), 0)
        pick = (slot == want).astype(jnp.float32).astype(jnp.bfloat16)
        moved = jnp.dot(pick, unit[...], preferred_element_type=jnp.float32)
        return moved.astype(jnp.bfloat16).reshape(2, SLOTS, width)

    def dispatch(j, _):
        off = nc // 2 + ((j + 1) // 2) * (1 - 2 * (j % 2))
        chip = (mine + off + nc) % nc
        send[pl.ds(2 * chip, 2)] = packed(chip)
        for h in range(2):
            d = 2 * chip + h
            unit_copy(d, me, d, me, d).start()
            key_copy(d, me, d, me, d).start()
        return 0

    lax.fori_loop(0, nc - 1, dispatch, 0)
    send[pl.ds(2 * mine, 2)] = packed(mine)
    unit_copy(mate, me, mate, me, mate).start()
    key_copy(mate, me, mate, me, mate).start()
    recv[me] = send[me]
    krecv[me] = ksend[me]

    def group_at(t):
        off = ((t + 1) // 2) * (2 * (t % 2) - 1)
        return (home + off + ng) % ng

    def units_of(g):
        return recv[pl.ds(q * g, q)].reshape(span, width)

    def turned(line):
        return jnp.transpose(jnp.broadcast_to(line, (LANES, line.shape[1])))

    def fold(x):
        return sum(x[:, c : c + LANES] for c in range(0, span, LANES))

    def step(t, _):
        g = group_at(t)
        for h in range(q):
            s = q * g + h

            @pl.when(s != me)
            def _():
                key_copy(s, s, s, s, s).wait_recv()
                unit_copy(s, s, s, s, s).wait_recv()

        tiles = [krecv[q * g + h] for h in range(q)]
        kc = jnp.concatenate([turned(x[0:1])[0:SLOTS] for x in tiles], axis=0)
        bc = jnp.concatenate([turned(x[4:5])[0:SLOTS] for x in tiles], axis=0)
        krow[t] = jnp.transpose(kc)[0:8]
        brow[t] = jnp.transpose(bc)[0:8]
        kc = jnp.concatenate([kc] * (span // LANES), axis=1)
        bc = jnp.concatenate([bc] * (span // LANES), axis=1)
        here = units_of(g)

        def pairs(u, gu):
            e = jnp.exp2(dot_nt(here, units_of(gu)) * SHARPNESS)
            e = jnp.where(bc == brow[u][0:1], e, 0.0)
            return e, jnp.where(krow[u][0:1] < kc, e, 0.0)

        _, lower = pairs(t, g)
        acc = fold(lower)

        def against(u, acc):
            e, lower = pairs(u, group_at(u))
            rowacc[u] = rowacc[u] + (e - lower).reshape(span // 8, 8, span).sum(axis=0)
            return acc + fold(lower)

        acc = lax.fori_loop(0, t, against, acc)
        total = jnp.broadcast_to(jnp.sum(acc, axis=1, keepdims=True), (span, LANES))
        as_row = jnp.transpose(total)[0:8, :]
        first = lax.broadcasted_iota(jnp.int32, (8, span), 0) == 0
        rowacc[t] = jnp.where(first, as_row, 0.0)
        return 0

    lax.fori_loop(0, ng, step, 0)

    def give_back(t, _):
        g = group_at(t)
        scores = turned(jnp.log1p(jnp.sum(rowacc[t], axis=0, keepdims=True)))
        for h in range(q):
            s = q * g + h
            chunk = scores[h * SLOTS : (h + 1) * SLOTS]
            if SLOTS < LANES:
                empty = jnp.zeros((LANES - SLOTS, LANES), jnp.float32)
                chunk = jnp.concatenate([chunk, empty], axis=0)
            ssend[s] = jnp.transpose(chunk)[0:8]

            @pl.when(s != me)
            def _():
                score_copy(s, me, s, me, s).start()

        return 0

    lax.fori_loop(0, ng, give_back, 0)
    ret[me] = ssend[me]

    def collect(k, _):
        s = (me + k) % n
        score_copy(s, s, s, s, s).wait_recv()
        return 0

    lax.fori_loop(1, n, collect, 0)

    back = ret[...][:, 0, :]
    hits_b = hits_f.astype(jnp.bfloat16)
    hi = back.astype(jnp.bfloat16)
    rest = back - hi.astype(jnp.float32)
    mid = rest.astype(jnp.bfloat16)
    low = (rest - mid.astype(jnp.float32)).astype(jnp.bfloat16)
    spread = sum(
        lax.dot_general(p, hits_b, (((0,), (0,)), ((), ())), preferred_element_type=jnp.float32)
        for p in (hi, mid, low)
    )
    out[...] = jnp.sum(jnp.where(at_slot, spread, 0.0), axis=0, keepdims=True)

    def drain(k, _):
        s = (me + k) % n
        unit_copy(s, s, s, s, s).wait_send()
        key_copy(s, s, s, s, s).wait_send()
        score_copy(s, s, s, s, s).wait_send()
        return 0

    lax.fori_loop(1, n, drain, 0)


def params(number):
    return pltpu.CompilerParams(
        collective_id=number, has_side_effects=True, vmem_limit_bytes=56 * 1024 * 1024
    )


def exchange(number, n, slots, q, rows, width):
    ng = n // q
    vmem = pl.BlockSpec(memory_space=pltpu.VMEM)
    dma = pltpu.SemaphoreType.DMA((n,))
    return pl.pallas_call(
        functools.partial(kernel, n, slots, q),
        out_shape=jax.ShapeDtypeStruct((1, rows), jnp.float32),
        in_specs=[vmem] * 5,
        out_specs=vmem,
        scratch_shapes=[
            pltpu.VMEM((n, slots, width), jnp.bfloat16),
            pltpu.VMEM((n, slots, width), jnp.bfloat16),
            pltpu.VMEM((n, 8, LANES), jnp.float32),
            pltpu.VMEM((n, 8, LANES), jnp.float32),
            pltpu.VMEM((ng, 8, q * slots), jnp.float32),
            pltpu.VMEM((ng, 8, q * slots), jnp.float32),
            pltpu.VMEM((ng, 8, q * slots), jnp.float32),
            pltpu.VMEM((n, 8, LANES), jnp.float32),
            pltpu.VMEM((n, 8, LANES), jnp.float32),
            dma, dma, dma, dma, dma, dma,
        ],
        compiler_params=params(number),
    )


def per_device(embeddings, owner_ids, local_cluster, arrival_rank):
    rows, width = embeddings.shape
    n = lax.axis_size("blk")
    groups = lax.axis_size("parts")
    vmem = pl.BlockSpec(memory_space=pltpu.VMEM)
    small = -(-3 * rows // (2 * n) // 32) * 32
    owner = owner_ids.reshape(1, rows)
    local = local_cluster.reshape(1, rows)
    rank = arrival_rank.reshape(1, rows)
    unit, target, most = pl.pallas_call(
        functools.partial(plan, n, groups),
        out_shape=(
            jax.ShapeDtypeStruct((rows, width), jnp.bfloat16),
            jax.ShapeDtypeStruct((1, rows), jnp.int32),
            jax.ShapeDtypeStruct((8, LANES), jnp.float32),
        ),
        in_specs=[vmem] * 3,
        out_specs=(vmem,) * 3,
        scratch_shapes=[
            pltpu.VMEM((n, n, LANES), jnp.float32),
            pltpu.VMEM((groups, 8, LANES), jnp.float32),
            pltpu.SemaphoreType.DMA((n,)),
            pltpu.SemaphoreType.DMA((n,)),
            pltpu.SemaphoreType.DMA((groups,)),
            pltpu.SemaphoreType.DMA((groups,)),
        ],
        compiler_params=params(0),
    )(embeddings, owner, local)
    scores = lax.cond(
        most[0, 0] <= small,
        lambda: exchange(1, n, small, 4, rows, width)(unit, target, owner, local, rank),
        lambda: exchange(2, n, LANES, 2, rows, width)(unit, owner, owner, local, rank),
    )
    return scores.reshape(rows)


def solution(mesh):
    return jax.shard_map(
        per_device,
        mesh=mesh,
        in_specs=(
            P(("parts", "blk"), None),
            P(("parts", "blk"), None),
            P(("parts", "blk")),
            P(("parts", "blk")),
        ),
        out_specs=P(("parts", "blk")),
        check_vma=False,
    )
```

time: 122 us -> 107 us (0.88)
  Pallas kernels: 121 us -> 104 us
    pallas_call x1 -> x2, Pallas kernels: 121 us -> 104 us  [the longest x1 87.8 us: per_device(): exchange(1, n, small, 4, rows, width)(unit, target, owner, local, rank)]
where the time goes in v2:
time: 107 us
  Pallas kernels  104 us (97%)
  local copies, waits for them, and re-layouts  1.8 us (2%)
    pallas_call x1, Pallas kernels, per_device(): exchange(1, n, small, 4, rows, width)(unit, target, owner, local, rank)  87.8 us
    pallas_call x1, Pallas kernels, per_device(): pl.pallas_call(functools.partial(plan, n, groups), out_shape=(jax.ShapeDt...  16.7 us

profile of v2, /device:TPU:0, one launch (start us, length us, event | category | flops | bytes accessed | tf_op | source)
XLA Modules:
  0.0 107.0 jit_solution(7335415599638316163)
XLA Ops:
  0.0 0.0 copy-start.2
  0.0 0.0 copy-start.1
  0.0 0.0 copy-start
  0.0 16.7 %shard_map.48 = (bf16[1024,1024]{1,0:T(8,128)(2,1)S(1)}, s32[1,1024]{1,0:T(1,128)S(1)}, f32[8,128]{1,0:T(8,128)}) custom-call(bf16[1024,1024]{1,0:T(8,128)(2,1)} %emb.1, s32[1,1024]{1,0:T(1,128)} %bitcast.6, s32[1,1024]{1,0:T(1,128)} %bitcast.9), custom_call_target="tpu_custom_call" | custom-call | tf_op jit(solution)/shard_map/pallas_call | solution.py:379
  16.7 1.2 %slice.3 = f32[1,1]{1,0:T(1,128)} slice(f32[8,128]{1,0:T(8,128)} %get-tuple-element.39), slice={[0:1], [0:1]} | slice | bytes 8 | tf_op jit(solution)/shard_map/slice | solution.py:399
  18.6 0.0 copy-done.2
  18.6 0.0 copy-done.1
  18.6 0.0 copy-done
  18.6 87.8 %conditional.1 = (f32[1024]{0:T(1024)S(1)}) conditional(s32[]{:T(128)} %bitcast.4, (bf16[1024,1024]{1,0:T(8,128)(2,1)S(1)}, s32[1,1024]{1,0:T(1,128)S(1)}, s32[1,1024]{1,0:T(1,128)S(1)}, s32[1,1024]{1,0:T(1,128)S(1)}) %tuple.23, (bf16[1024,1024]{1,0:T(8,128)(2,1)S(1)}, s32[1,1024]{1,0:T(1,128)S(1)}, s32[1,1024]{1,0:T(1,128)S(1)}, ...), branch_computations={%region_0.0_spmd, %region_1.0_spmd} | conditional | bytes 8 | solution.py:398
  18.6 87.8 %branch_1_fun.1 = f32[1,1024]{1,0:T(1,128)S(1)} custom-call(bf16[1024,1024]{1,0:T(8,128)(2,1)S(1)} %get-tuple-element.31.unit, s32[1,1024]{1,0:T(1,128)S(1)} %get-tuple-element.32.tgt, s32[1,1024]{1,0:T(1,128)S(1)} %get-tuple-element.33.own, s32[1,1024]{1,0:T(1,128)S(1)} %get-tuple-element.34.lc, s32[1,1024]{1,0:T(1,128)S(1)} %get-tuple-element.35.rank), custom_call_target="tpu_custom_call" | custom-call | tf_op jit(solution)/shard_map/cond/branch_1_fun/pallas_call | solution.py:400
  106.4 0.6 copy.10
Async XLA Ops:
  0.0 18.6 %copy-start.2 = (s32[1024]{0:T(1024)S(1)}, s32[1024]{0:T(1024)}, u32[]{:S(2)}) copy-start(s32[1024]{0:T(1024)} %param.9) | copy-start | bytes 12292
  0.0 18.6 %copy-start.1 = (s32[1024]{0:T(1024)S(1)}, s32[1024]{0:T(1024)}, u32[]{:S(2)}) copy-start(s32[1024]{0:T(1024)} %param.8) | copy-start | bytes 12292
  0.0 18.6 %copy-start = (s32[1024,1]{0,1:T(1,128)S(1)}, s32[1024,1]{0,1:T(1,128)}, u32[]{:S(2)}) copy-start(s32[1024,1]{0,1:T(1,128)} %param.7) | copy-start | bytes 12292

commit v3 on v2

--- a/solution.py
+++ b/solution.py
@@ -39,7 +39,7 @@
     return total
 
 
-def plan(n, groups, emb, own, lc, unit, tgt, most, cnt, tops, cs, cr, ts, tr):
+def plan(n, groups, near, far, emb, own, lc, unit, tgt, most, cnt, tops, cs, cr, ts, tr):
     rows = emb.shape[0]
     me = lax.axis_index("blk")
     part = lax.axis_index("parts")
@@ -92,22 +92,42 @@
 
     lax.fori_loop(1, n, take_counts, 0)
 
+    half = n // 2
     total = jnp.sum(cnt[...], axis=0)
-    inside = exact_dot(total, narrow(below(LANES).astype(jnp.float32)))
-    sums = jnp.broadcast_to(jnp.sum(total, axis=1, keepdims=True), (n, LANES))
-    ahead = jnp.zeros((n, LANES), jnp.float32)
+    lean = total - 2.0 * jnp.sum(cnt[0:half], axis=0)
     line = lax.broadcasted_iota(jnp.int32, (n, LANES), 0)
-    for o in range(n - 1):
-        ahead = ahead + jnp.where(line > o, sums[o : o + 1], 0.0)
-    middle = inside + ahead + 0.5 * total
-    dest = jnp.minimum(jnp.floor(middle * (1.0 / rows)), float(n - 1))
+    number = line * CL_DEV + lax.broadcasted_iota(jnp.int32, (n, LANES), 1)
+    lean = lean + ((number * 7) % 16).astype(jnp.float32) * 0.0625
+
+    def whole(x):
+        return jnp.sum(jnp.sum(x, axis=0, keepdims=True), axis=1, keepdims=True)
+
+    edge = jnp.full((1, 1), -4.0, jnp.float32)
+    for move in (4.0, 2.0, 1.0, 0.5, 0.25, 0.125, 0.0625):
+        upper = whole(jnp.where(lean > edge + move, total, 0.0))
+        edge = jnp.where(upper > 0.5 * n * rows, edge + move, edge)
+    high = lean > edge
+    dest = jnp.zeros((n, LANES), jnp.float32)
+    for chosen, start in ((high, half), (jnp.logical_not(high), 0)):
+        mass = jnp.where(chosen, total, 0.0)
+        inside = exact_dot(mass, narrow(below(LANES).astype(jnp.float32)))
+        sums = jnp.broadcast_to(jnp.sum(mass, axis=1, keepdims=True), (n, LANES))
+        ahead = jnp.zeros((n, LANES), jnp.float32)
+        for o in range(n - 1):
+            ahead = ahead + jnp.where(line > o, sums[o : o + 1], 0.0)
+        scale = half / jnp.maximum(whole(mass), 1.0)
+        index = jnp.floor((inside + ahead + 0.5 * mass) * scale)
+        dest = jnp.where(chosen, jnp.minimum(index, half - 1.0) + float(start), dest)
+
+    source = lax.broadcasted_iota(jnp.int32, (n, 1), 0) // half
 
     def widest(d, top):
         mask = (dest == d.astype(jnp.float32)).astype(jnp.float32)
-        per_src = jnp.sum(cnt[...] * mask[None], axis=1)
-        return jnp.maximum(top, jnp.sum(per_src, axis=1, keepdims=True))
-
-    top = lax.fori_loop(0, n, widest, jnp.zeros((n, 1), jnp.float32))
+        per_src = jnp.sum(jnp.sum(cnt[...] * mask[None], axis=1), axis=1, keepdims=True)
+        room = jnp.where(source == d // half, float(near), float(far))
+        return jnp.maximum(top, per_src - room)
+
+    top = lax.fori_loop(0, n, widest, jnp.full((n, 1), -float(rows), jnp.float32))
     top = jnp.broadcast_to(jnp.max(top, axis=0, keepdims=True), (8, LANES))
 
     tops[part] = top
@@ -142,18 +162,20 @@
 
 
 def kernel(
-    n, SLOTS, q, unit, tgt, own, lc, rank, out,
-    send, recv, ksend, krecv, krow, brow, rowacc, ssend, ret,
+    n, near, far, tile, unit, tgt, own, lc, rank, out,
+    send, recv_near, recv_far, ksend, krecv, kc_near, bc_near, kc_far, bc_far,
+    acc_near, col_far, ssend, ret,
     us, ur, ks, kr, rs, rr,
 ):
     rows, width = unit.shape
     nc = n // 2
-    ng = n // q
-    PAIR = 2 * SLOTS
-    span = q * SLOTS
+    half = n // 2
+    hc = half // 2
     me = lax.axis_index("blk")
-    mine = me // 2
-    home = me // q
+    here = me % half
+    mine = here // 2
+    base_near = me - here
+    base_far = half - base_near
     mate = me + 1 - 2 * (me % 2)
 
     barrier = pltpu.get_barrier_semaphore()
@@ -172,7 +194,7 @@
         narrow(hits_f), narrow(below(rows).astype(jnp.float32)), preferred_element_type=jnp.float32
     )
     pos = jnp.sum(hits_f * earlier, axis=0, keepdims=True).astype(jnp.int32)
-    slot = target * SLOTS + pos
+    slot = target * LANES + pos
     at_slot, at_slot_f = one_hot(pos, LANES)
 
     rank_v = rank[...]
@@ -194,9 +216,11 @@
             device_id={"blk": dev}, device_id_type=MESH,
         )
 
-    def unit_copy(src, dst, send_at, recv_at, dev):
+    def unit_copy(src, dst, send_at, recv_at, dev, close):
+        room = near if close else far
+        into = recv_near if close else recv_far
         return pltpu.make_async_remote_copy(
-            src_ref=send.at[src], dst_ref=recv.at[dst],
+            src_ref=send.at[src, pl.ds(0, room)], dst_ref=into.at[dst],
             send_sem=us.at[send_at], recv_sem=ur.at[recv_at],
             device_id={"blk": dev}, device_id_type=MESH,
         )
@@ -210,101 +234,132 @@
 
     pl.semaphore_wait(barrier, n - 1)
 
-    def packed(chip):
-        want = chip * PAIR + lax.broadcasted_iota(jnp.int32, (PAIR, rows), 0)
-        pick = (slot == want).astype(jnp.float32).astype(jnp.bfloat16)
+    def send_keys(k, _):
+        d = (me + k) % n
+        key_copy(d, me, d, me, d).start()
+        return 0
+
+    lax.fori_loop(1, n, send_keys, 0)
+
+    def pack(first):
+        want = first * LANES + lax.broadcasted_iota(jnp.int32, (2 * LANES, rows), 0)
+        pick = narrow((slot == want).astype(jnp.float32))
         moved = jnp.dot(pick, unit[...], preferred_element_type=jnp.float32)
-        return moved.astype(jnp.bfloat16).reshape(2, SLOTS, width)
-
-    def dispatch(j, _):
-        off = nc // 2 + ((j + 1) // 2) * (1 - 2 * (j % 2))
-        chip = (mine + off + nc) % nc
-        send[pl.ds(2 * chip, 2)] = packed(chip)
+        send[pl.ds(first, 2)] = narrow(moved).reshape(2, LANES, width)
+
+    def dispatch_far(j, _):
+        first = base_far + 2 * ((mine + j) % hc)
+        pack(first)
         for h in range(2):
-            d = 2 * chip + h
-            unit_copy(d, me, d, me, d).start()
-            key_copy(d, me, d, me, d).start()
-        return 0
-
-    lax.fori_loop(0, nc - 1, dispatch, 0)
-    send[pl.ds(2 * mine, 2)] = packed(mine)
-    unit_copy(mate, me, mate, me, mate).start()
-    key_copy(mate, me, mate, me, mate).start()
-    recv[me] = send[me]
+            unit_copy(first + h, here, first + h, me, first + h, False).start()
+        return 0
+
+    def dispatch_near(j, _):
+        first = base_near + 2 * ((mine + j) % hc)
+        pack(first)
+        for h in range(2):
+            unit_copy(first + h, here, first + h, me, first + h, True).start()
+        return 0
+
+    lax.fori_loop(0, hc, dispatch_far, 0)
+    lax.fori_loop(1, hc, dispatch_near, 0)
+    pack(base_near + 2 * mine)
+    unit_copy(mate, here, mate, me, mate, True).start()
+    recv_near[here] = send[me, 0:near]
     krecv[me] = ksend[me]
 
-    def group_at(t):
-        off = ((t + 1) // 2) * (2 * (t % 2) - 1)
-        return (home + off + ng) % ng
-
-    def units_of(g):
-        return recv[pl.ds(q * g, q)].reshape(span, width)
+    def take_keys(k, _):
+        s = (me + k) % n
+        key_copy(s, s, s, s, s).wait_recv()
+        return 0
+
+    lax.fori_loop(1, n, take_keys, 0)
 
     def turned(line):
         return jnp.transpose(jnp.broadcast_to(line, (LANES, line.shape[1])))
 
+    def keys(base, room, kc, bc):
+        for h in range(half):
+            x = krecv[base + h]
+            kc[h * room : (h + 1) * room] = turned(x[0:1])[0:room]
+            bc[h * room : (h + 1) * room] = turned(x[4:5])[0:room]
+        return jnp.transpose(kc[...])[0:1], jnp.transpose(bc[...])[0:1]
+
+    kr_near, br_near = keys(base_near, near, kc_near, bc_near)
+    kr_far, br_far = keys(base_far, far, kc_far, bc_far)
+
+    def wide(x, lanes):
+        return jnp.concatenate([x] * (lanes // LANES), axis=1)
+
     def fold(x):
-        return sum(x[:, c : c + LANES] for c in range(0, span, LANES))
-
-    def step(t, _):
-        g = group_at(t)
-        for h in range(q):
-            s = q * g + h
-
-            @pl.when(s != me)
-            def _():
-                key_copy(s, s, s, s, s).wait_recv()
-                unit_copy(s, s, s, s, s).wait_recv()
-
-        tiles = [krecv[q * g + h] for h in range(q)]
-        kc = jnp.concatenate([turned(x[0:1])[0:SLOTS] for x in tiles], axis=0)
-        bc = jnp.concatenate([turned(x[4:5])[0:SLOTS] for x in tiles], axis=0)
-        krow[t] = jnp.transpose(kc)[0:8]
-        brow[t] = jnp.transpose(bc)[0:8]
-        kc = jnp.concatenate([kc] * (span // LANES), axis=1)
-        bc = jnp.concatenate([bc] * (span // LANES), axis=1)
-        here = units_of(g)
-
-        def pairs(u, gu):
-            e = jnp.exp2(dot_nt(here, units_of(gu)) * SHARPNESS)
-            e = jnp.where(bc == brow[u][0:1], e, 0.0)
-            return e, jnp.where(krow[u][0:1] < kc, e, 0.0)
-
-        _, lower = pairs(t, g)
-        acc = fold(lower)
-
-        def against(u, acc):
-            e, lower = pairs(u, group_at(u))
-            rowacc[u] = rowacc[u] + (e - lower).reshape(span // 8, 8, span).sum(axis=0)
-            return acc + fold(lower)
-
-        acc = lax.fori_loop(0, t, against, acc)
-        total = jnp.broadcast_to(jnp.sum(acc, axis=1, keepdims=True), (span, LANES))
-        as_row = jnp.transpose(total)[0:8, :]
-        first = lax.broadcasted_iota(jnp.int32, (8, span), 0) == 0
-        rowacc[t] = jnp.where(first, as_row, 0.0)
-        return 0
-
-    lax.fori_loop(0, ng, step, 0)
-
-    def give_back(t, _):
-        g = group_at(t)
-        scores = turned(jnp.log1p(jnp.sum(rowacc[t], axis=0, keepdims=True)))
-        for h in range(q):
-            s = q * g + h
-            chunk = scores[h * SLOTS : (h + 1) * SLOTS]
-            if SLOTS < LANES:
-                empty = jnp.zeros((LANES - SLOTS, LANES), jnp.float32)
-                chunk = jnp.concatenate([chunk, empty], axis=0)
-            ssend[s] = jnp.transpose(chunk)[0:8]
-
-            @pl.when(s != me)
-            def _():
-                score_copy(s, me, s, me, s).start()
-
-        return 0
-
-    lax.fori_loop(0, ng, give_back, 0)
+        return sum(x[:, c : c + LANES] for c in range(0, x.shape[1], LANES))
+
+    def down(x):
+        return x.reshape(x.shape[0] // 8, 8, x.shape[1]).sum(axis=0)
+
+    def pairs(recv, p, room, kc, bc, other, kr, br):
+        lanes = other.shape[0] * other.shape[1]
+        left = recv[pl.ds(tile * p, tile)].reshape(tile * room, width)
+        at = pl.ds(pl.multiple_of(p * (tile * room), 16), tile * room)
+        e = jnp.exp2(dot_nt(left, other[...].reshape(lanes, width)) * SHARPNESS)
+        e = jnp.where(wide(bc[at], lanes) == br, e, 0.0)
+        return at, e, wide(kc[at], lanes) < kr
+
+    def wait_near(k, _):
+        s = (here + k) % half
+        d = base_near + s
+        unit_copy(d, s, d, d, d, True).wait_recv()
+        return 0
+
+    lax.fori_loop(1, half, wait_near, 0)
+
+    def near_near(p, acc):
+        _, e, before = pairs(recv_near, p, near, kc_near, bc_near, recv_near, kr_near, br_near)
+        return acc + down(jnp.where(before, e, 0.0))
+
+    acc_near[...] = lax.fori_loop(
+        0, half // tile, near_near, jnp.zeros((8, half * near), jnp.float32)
+    )
+
+    def far_near(j, _):
+        p = (here // tile - j + half // tile) % (half // tile)
+        for h in range(tile):
+            s = tile * p + h
+            d = base_far + s
+            unit_copy(d, s, d, d, d, False).wait_recv()
+        at, e, before = pairs(recv_far, p, far, kc_far, bc_far, recv_near, kr_near, br_near)
+        lower = jnp.where(before, e, 0.0)
+        acc_near[...] = acc_near[...] + down(lower)
+        sums = jnp.sum(fold(e - lower), axis=1, keepdims=True)
+        col_far[at] = jnp.broadcast_to(sums, (tile * far, LANES))
+        return 0
+
+    lax.fori_loop(0, half // tile, far_near, 0)
+
+    def give_back(h, base, column):
+        s = base + h
+        room = column.shape[0]
+        if room < LANES:
+            empty = jnp.zeros((LANES - room, LANES), jnp.float32)
+            column = jnp.concatenate([column, empty], axis=0)
+        ssend[s] = jnp.transpose(column)[0:8]
+
+        @pl.when(s != me)
+        def _():
+            score_copy(s, me, s, me, s).start()
+
+    scores = turned(jnp.log1p(jnp.sum(acc_near[...], axis=0, keepdims=True)))
+    for h in range(half):
+        give_back(h, base_near, scores[h * near : (h + 1) * near])
+
+    def far_far(p, acc):
+        _, e, before = pairs(recv_far, p, far, kc_far, bc_far, recv_far, kr_far, br_far)
+        return acc + down(jnp.where(before, e, 0.0))
+
+    acc = lax.fori_loop(0, half // tile, far_far, jnp.zeros((8, half * far), jnp.float32))
+    scores = jnp.log1p(turned(jnp.sum(acc, axis=0, keepdims=True)) + col_far[...])
+    for h in range(half):
+        give_back(h, base_far, scores[h * far : (h + 1) * far])
     ret[me] = ssend[me]
 
     def collect(k, _):
@@ -328,12 +383,24 @@
 
     def drain(k, _):
         s = (me + k) % n
-        unit_copy(s, s, s, s, s).wait_send()
         key_copy(s, s, s, s, s).wait_send()
         score_copy(s, s, s, s, s).wait_send()
         return 0
 
+    def drain_near(k, _):
+        s = (here + k) % half
+        d = base_near + s
+        unit_copy(d, s, d, d, d, True).wait_send()
+        return 0
+
+    def drain_far(s, _):
+        d = base_far + s
+        unit_copy(d, s, d, d, d, False).wait_send()
+        return 0
+
     lax.fori_loop(1, n, drain, 0)
+    lax.fori_loop(1, half, drain_near, 0)
+    lax.fori_loop(0, half, drain_far, 0)
 
 
 def params(number):
@@ -342,23 +409,28 @@
     )
 
 
-def exchange(number, n, slots, q, rows, width):
-    ng = n // q
+def exchange(number, n, near, far, rows, width):
+    half = n // 2
+    tile = 2 if half * near <= 1024 else 1
     vmem = pl.BlockSpec(memory_space=pltpu.VMEM)
     dma = pltpu.SemaphoreType.DMA((n,))
     return pl.pallas_call(
-        functools.partial(kernel, n, slots, q),
+        functools.partial(kernel, n, near, far, tile),
         out_shape=jax.ShapeDtypeStruct((1, rows), jnp.float32),
         in_specs=[vmem] * 5,
         out_specs=vmem,
         scratch_shapes=[
-            pltpu.VMEM((n, slots, width), jnp.bfloat16),
-            pltpu.VMEM((n, slots, width), jnp.bfloat16),
+            pltpu.VMEM((n, LANES, width), jnp.bfloat16),
+            pltpu.VMEM((half, near, width), jnp.bfloat16),
+            pltpu.VMEM((half, far, width), jnp.bfloat16),
             pltpu.VMEM((n, 8, LANES), jnp.float32),
             pltpu.VMEM((n, 8, LANES), jnp.float32),
-            pltpu.VMEM((ng, 8, q * slots), jnp.float32),
-            pltpu.VMEM((ng, 8, q * slots), jnp.float32),
-            pltpu.VMEM((ng, 8, q * slots), jnp.float32),
+            pltpu.VMEM((half * near, LANES), jnp.float32),
+            pltpu.VMEM((half * near, LANES), jnp.float32),
+            pltpu.VMEM((half * far, LANES), jnp.float32),
+            pltpu.VMEM((half * far, LANES), jnp.float32),
+            pltpu.VMEM((8, half * near), jnp.float32),
+            pltpu.VMEM((half * far, LANES), jnp.float32),
             pltpu.VMEM((n, 8, LANES), jnp.float32),
             pltpu.VMEM((n, 8, LANES), jnp.float32),
             dma, dma, dma, dma, dma, dma,
@@ -372,12 +444,13 @@
     n = lax.axis_size("blk")
     groups = lax.axis_size("parts")
     vmem = pl.BlockSpec(memory_space=pltpu.VMEM)
-    small = -(-3 * rows // (2 * n) // 32) * 32
+    near = min(LANES, -(-7 * rows // (4 * n) // 16) * 16)
+    far = min(LANES, -(-5 * rows // (4 * n) // 16) * 16)
     owner = owner_ids.reshape(1, rows)
     local = local_cluster.reshape(1, rows)
     rank = arrival_rank.reshape(1, rows)
     unit, target, most = pl.pallas_call(
-        functools.partial(plan, n, groups),
+        functools.partial(plan, n, groups, near, far),
         out_shape=(
             jax.ShapeDtypeStruct((rows, width), jnp.bfloat16),
             jax.ShapeDtypeStruct((1, rows), jnp.int32),
@@ -396,9 +469,9 @@
         compiler_params=params(0),
     )(embeddings, owner, local)
     scores = lax.cond(
-        most[0, 0] <= small,
-        lambda: exchange(1, n, small, 4, rows, width)(unit, target, owner, local, rank),
-        lambda: exchange(2, n, LANES, 2, rows, width)(unit, owner, owner, local, rank),
+        most[0, 0] <= 0.0,
+        lambda: exchange(1, n, near, far, rows, width)(unit, target, owner, local, rank),
+        lambda: exchange(2, n, LANES, LANES, rows, width)(unit, owner, owner, local, rank),
     )
     return scores.reshape(rows)
 

time: 107 us -> 96.3 us (0.900)
  Pallas kernels: 104 us -> 93.6 us
    pallas_call x2, Pallas kernels: 104 us -> 93.6 us  [the longest x1 76.2 us: per_device(): exchange(1, n, near, far, rows, width)(unit, target, owner, local, rank)]
where the time goes in v3:
time: 96.3 us; the launch traced here: 96.1 us
  Pallas kernels  93.6 us (97%)
  local copies, waits for them, and re-layouts  1.8 us (2%)
    pallas_call x1, Pallas kernels, per_device(): exchange(1, n, near, far, rows, width)(unit, target, owner, local, rank)  76.2 us
    pallas_call x1, Pallas kernels, per_device(): pl.pallas_call(functools.partial(plan, n, groups, near, far), out_shape=(...  17.4 us

profile of v3, /device:TPU:0, one launch (start us, length us, event | category | flops | bytes accessed | tf_op | source)
XLA Modules:
  0.0 96.1 jit_solution(7151706596213169007)
XLA Ops:
  0.0 0.0 copy-start.2
  0.0 0.0 copy-start.1
  0.0 0.0 copy-start
  0.0 17.4 %shard_map.48 = (bf16[1024,1024]{1,0:T(8,128)(2,1)S(1)}, s32[1,1024]{1,0:T(1,128)S(1)}, f32[8,128]{1,0:T(8,128)}) custom-call(bf16[1024,1024]{1,0:T(8,128)(2,1)} %emb.1, s32[1,1024]{1,0:T(1,128)} %bitcast.6, s32[1,1024]{1,0:T(1,128)} %bitcast.9), custom_call_target="tpu_custom_call" | custom-call | tf_op jit(solution)/shard_map/pallas_call | solution.py:452
  17.4 1.2 %slice.3 = f32[1,1]{1,0:T(1,128)} slice(f32[8,128]{1,0:T(8,128)} %get-tuple-element.39), slice={[0:1], [0:1]} | slice | bytes 8 | tf_op jit(solution)/shard_map/slice | solution.py:472
  19.2 0.0 copy-done.2
  19.2 0.0 copy-done.1
  19.2 0.0 copy-done
  19.3 76.2 %conditional.1 = (f32[1024]{0:T(1024)S(1)}) conditional(s32[]{:T(128)} %bitcast.4, (bf16[1024,1024]{1,0:T(8,128)(2,1)S(1)}, s32[1,1024]{1,0:T(1,128)S(1)}, s32[1,1024]{1,0:T(1,128)S(1)}, s32[1,1024]{1,0:T(1,128)S(1)}) %tuple.23, (bf16[1024,1024]{1,0:T(8,128)(2,1)S(1)}, s32[1,1024]{1,0:T(1,128)S(1)}, s32[1,1024]{1,0:T(1,128)S(1)}, ...), branch_computations={%region_0.0_spmd, %region_1.0_spmd} | conditional | bytes 8 | solution.py:471
  19.3 76.2 %branch_1_fun.1 = f32[1,1024]{1,0:T(1,128)S(1)} custom-call(bf16[1024,1024]{1,0:T(8,128)(2,1)S(1)} %get-tuple-element.31.unit, s32[1,1024]{1,0:T(1,128)S(1)} %get-tuple-element.32.tgt, s32[1,1024]{1,0:T(1,128)S(1)} %get-tuple-element.33.own, s32[1,1024]{1,0:T(1,128)S(1)} %get-tuple-element.34.lc, s32[1,1024]{1,0:T(1,128)S(1)} %get-tuple-element.35.rank), custom_call_target="tpu_custom_call" | custom-call | tf_op jit(solution)/shard_map/cond/branch_1_fun/pallas_call | solution.py:473
  95.5 0.6 copy.10
Async XLA Ops:
  0.0 19.2 %copy-start.2 = (s32[1024]{0:T(1024)S(1)}, s32[1024]{0:T(1024)}, u32[]{:S(2)}) copy-start(s32[1024]{0:T(1024)} %param.9) | copy-start | bytes 12292
  0.0 19.2 %copy-start.1 = (s32[1024]{0:T(1024)S(1)}, s32[1024]{0:T(1024)}, u32[]{:S(2)}) copy-start(s32[1024]{0:T(1024)} %param.8) | copy-start | bytes 12292
  0.0 19.2 %copy-start = (s32[1024,1]{0,1:T(1,128)S(1)}, s32[1024,1]{0,1:T(1,128)}, u32[]{:S(2)}) copy-start(s32[1024,1]{0,1:T(1,128)} %param.7) | copy-start | bytes 12292

commit v4 on v3

--- a/solution.py
+++ b/solution.py
@@ -119,16 +119,17 @@
         index = jnp.floor((inside + ahead + 0.5 * mass) * scale)
         dest = jnp.where(chosen, jnp.minimum(index, half - 1.0) + float(start), dest)
 
-    source = lax.broadcasted_iota(jnp.int32, (n, 1), 0) // half
-
-    def widest(d, top):
-        mask = (dest == d.astype(jnp.float32)).astype(jnp.float32)
-        per_src = jnp.sum(jnp.sum(cnt[...] * mask[None], axis=1), axis=1, keepdims=True)
-        room = jnp.where(source == d // half, float(near), float(far))
-        return jnp.maximum(top, per_src - room)
-
-    top = lax.fori_loop(0, n, widest, jnp.full((n, 1), -float(rows), jnp.float32))
-    top = jnp.broadcast_to(jnp.max(top, axis=0, keepdims=True), (8, LANES))
+    by_owner = jnp.transpose(cnt[...], (1, 0, 2))
+    device = lax.broadcasted_iota(jnp.int32, (n, LANES), 0).astype(jnp.float32)
+    load = jnp.zeros((n, n), jnp.float32)
+    for o in range(n):
+        mask = (dest[o : o + 1] == device).astype(jnp.float32)
+        load = load + dot_nt(narrow(by_owner[o]), narrow(mask))
+    source = lax.broadcasted_iota(jnp.int32, (n, n), 0) // half
+    place = lax.broadcasted_iota(jnp.int32, (n, n), 1) // half
+    over = load - jnp.where(source == place, float(near), float(far))
+    top = jnp.max(jnp.max(over, axis=0, keepdims=True), axis=1, keepdims=True)
+    top = jnp.broadcast_to(top, (8, LANES))
 
     tops[part] = top
 
@@ -149,7 +150,7 @@
 
     for d in others:
         top_copy(d, d, d, d).wait_recv()
-    most[...] = jnp.max(tops[...], axis=0)
+    most[0, 0] = jnp.max(tops[...])
     for d in others:
         top_copy(d, d, d, d).wait_send()
 
@@ -454,10 +455,10 @@
         out_shape=(
             jax.ShapeDtypeStruct((rows, width), jnp.bfloat16),
             jax.ShapeDtypeStruct((1, rows), jnp.int32),
-            jax.ShapeDtypeStruct((8, LANES), jnp.float32),
+            jax.ShapeDtypeStruct((1, 1), jnp.float32),
         ),
         in_specs=[vmem] * 3,
-        out_specs=(vmem,) * 3,
+        out_specs=(vmem, vmem, pl.BlockSpec(memory_space=pltpu.SMEM)),
         scratch_shapes=[
             pltpu.VMEM((n, n, LANES), jnp.float32),
             pltpu.VMEM((groups, 8, LANES), jnp.float32),

time: 96.3 us -> 93.6 us (0.972)
  Pallas kernels: 93.6 us -> 92.1 us
  local copies, waits for them, and re-layouts: 1.8 us -> 0.61 us
    pallas_call x1, Pallas kernels: 17.4 us -> 15.9 us  [per_device(): pl.pallas_call(functools.partial(plan, n, groups, near, far), out_shape=(...]
    slice x1 -> x0, local copies, waits for them, and re-layouts: 1.19 us -> none  [per_device(): most[0, 0] <= 0.0]
where the time goes in v4:
time: 93.6 us; the launch traced here: 93.5 us
  Pallas kernels  92.1 us (98%)
    pallas_call x1, Pallas kernels, per_device(): exchange(1, n, near, far, rows, width)(unit, target, owner, local, rank)  76.2 us
    pallas_call x1, Pallas kernels, per_device(): pl.pallas_call(functools.partial(plan, n, groups, near, far), out_shape=(...  15.9 us

profile of v4, /device:TPU:0, one launch (start us, length us, event | category | flops | bytes accessed | tf_op | source)
XLA Modules:
  0.0 93.5 jit_solution(8721699313466940294)
XLA Ops:
  0.0 0.0 copy-start.2
  0.0 0.0 copy-start.1
  0.0 0.0 copy-start
  0.0 15.9 %shard_map.48 = (bf16[1024,1024]{1,0:T(8,128)(2,1)S(1)}, s32[1,1024]{1,0:T(1,128)S(1)}, f32[1,1]{1,0:T(1,128)}) custom-call(bf16[1024,1024]{1,0:T(8,128)(2,1)} %emb.1, s32[1,1024]{1,0:T(1,128)} %bitcast.6, s32[1,1024]{1,0:T(1,128)} %bitcast.9), custom_call_target="tpu_custom_call" | custom-call | tf_op jit(solution)/shard_map/pallas_call | solution.py:453
  16.6 0.0 copy-done.2
  16.6 0.0 copy-done.1
  16.7 0.0 copy-done
  16.7 76.2 %conditional.1 = (f32[1024]{0:T(1024)S(1)}) conditional(s32[]{:T(128)} %bitcast.4, (bf16[1024,1024]{1,0:T(8,128)(2,1)S(1)}, s32[1,1024]{1,0:T(1,128)S(1)}, s32[1,1024]{1,0:T(1,128)S(1)}, s32[1,1024]{1,0:T(1,128)S(1)}) %tuple.23, (bf16[1024,1024]{1,0:T(8,128)(2,1)S(1)}, s32[1,1024]{1,0:T(1,128)S(1)}, s32[1,1024]{1,0:T(1,128)S(1)}, ...), branch_computations={%region_0.0_spmd, %region_1.0_spmd} | conditional | bytes 8 | solution.py:472
  16.7 76.2 %branch_1_fun.1 = f32[1,1024]{1,0:T(1,128)S(1)} custom-call(bf16[1024,1024]{1,0:T(8,128)(2,1)S(1)} %get-tuple-element.31.unit, s32[1,1024]{1,0:T(1,128)S(1)} %get-tuple-element.32.tgt, s32[1,1024]{1,0:T(1,128)S(1)} %get-tuple-element.33.own, s32[1,1024]{1,0:T(1,128)S(1)} %get-tuple-element.34.lc, s32[1,1024]{1,0:T(1,128)S(1)} %get-tuple-element.35.rank), custom_call_target="tpu_custom_call" | custom-call | tf_op jit(solution)/shard_map/cond/branch_1_fun/pallas_call | solution.py:474
  92.9 0.6 copy.10
Async XLA Ops:
  0.0 16.6 %copy-start.2 = (s32[1024]{0:T(1024)S(1)}, s32[1024]{0:T(1024)}, u32[]{:S(2)}) copy-start(s32[1024]{0:T(1024)} %param.9) | copy-start | bytes 12292
  0.0 16.6 %copy-start.1 = (s32[1024]{0:T(1024)S(1)}, s32[1024]{0:T(1024)}, u32[]{:S(2)}) copy-start(s32[1024]{0:T(1024)} %param.8) | copy-start | bytes 12292
  0.0 16.7 %copy-start = (s32[1024,1]{0,1:T(1,128)S(1)}, s32[1024,1]{0,1:T(1,128)}, u32[]{:S(2)}) copy-start(s32[1024,1]{0,1:T(1,128)} %param.7) | copy-start | bytes 12292
